TPU v7x, 128 devices: a whole 4x4x4 slice. The times are simulated.
128 devices in a mesh: dp: 4 (over x), leaf: 32 (over z, y, core).
Axes of the slice: x: 4, y: 4, z: 4, core: 2. Of those that a mesh axis runs over, the one named last changes fastest.
Arguments:
- queries: bfloat16 [32768, 3584], P(('dp', 'leaf')), may hold values from -72 to 72
- branch_keys: bfloat16 [32768, 512], P(('dp', 'leaf')), may hold values from -6 to 6
- branch_value_rows: bfloat16 [32768, 512], P(('dp', 'leaf')), may hold values from -6 to 6
- attention_output: bfloat16 [32768, 3584], P(('dp', 'leaf')), may hold values from -1.75 to 1.75
- output_gradient: bfloat16 [32768, 3584], P(('dp', 'leaf')), may hold values from -96 to 96
- anc_states: bfloat16 [16384, 3584], P(('dp', 'leaf')), may hold values from -24 to 24
- key_matrix: bfloat16 [3584, 512], replicated, may hold values from -0.09375 to 0.09375
- value_matrix: bfloat16 [3584, 512], replicated, may hold values from -0.09375 to 0.09375
- anc_blocks: int32 [128, 16], P(('dp', 'leaf')), may hold values from 0 to 63, as said below
- anc_count: int32 [128], P(('dp', 'leaf')), may hold values from 12 to 16, as said below
Outputs:
- query_grad: bfloat16 [32768, 3584], P(('dp', 'leaf'))
- branch_key_grad: bfloat16 [32768, 512], P(('dp', 'leaf'))
- branch_value_grad: bfloat16 [32768, 512], P(('dp', 'leaf'))
- anc_state_grad: bfloat16 [16384, 3584], P(('dp', 'leaf'))
- key_weight_grad: float32 [3584, 512], P(('dp', 'leaf'))
- value_weight_grad: float32 [3584, 512], P(('dp', 'leaf'))
Inputs may be any that keep to these rules, and one draw needn't show every extreme that they name: `anc_blocks`: block b of a dp group is held by leaf index b // 2 of that group as its local block b % 2. The 16 entries of one device are distinct, and at most 1 of them are held by one leaf index. Slots 0 to anc_count - 1 of a device's list are live, the others are ignored. In every dp group some device has 16 live slots.
All inputs are finite; a program needn't handle non-finite values.
Results may differ from a plain program's by a relative error of at most 0.022.
Values may be sent and summed in bfloat16 or wider, within the bound.
A program may use at most 192 MiB of HBM per device.

v0:
```python
import math

import jax
import jax.numpy as jnp
from jax import lax
from jax.sharding import PartitionSpec as P

QUERY_HEADS = 28
KEY_VALUE_HEADS = 4
HEAD_SIZE = 128
NA = 16
BLK = 64


def contract_rows(left, right):
    return lax.dot_general(
        left, right, (((0,), (0,)), ((), ())), preferred_element_type=jnp.float32
    )


def contract_cols(left, right):
    return lax.dot_general(
        left, right, (((1,), (1,)), ((), ())), preferred_element_type=jnp.float32
    )


def attend(queries, key_tokens, values, attention_output, output_gradient, key_live):
    group_width = QUERY_HEADS // KEY_VALUE_HEADS
    query_tokens = queries.shape[0]
    key_count = key_tokens.shape[0]
    anc_keys = key_count - query_tokens
    score_scale = 1.0 / math.sqrt(HEAD_SIZE)
    row_tok = jnp.arange(query_tokens * group_width, dtype=jnp.int32) // group_width
    key_pos = jnp.arange(key_count, dtype=jnp.int32)
    causal = key_pos[None, :] - anc_keys <= row_tok[:, None]
    visible = jnp.where(key_pos[None, :] < anc_keys, key_live[None, :], causal)
    query_head_rows = queries.reshape(query_tokens, KEY_VALUE_HEADS, group_width * HEAD_SIZE)
    output_heads = attention_output.reshape(query_tokens, KEY_VALUE_HEADS, group_width * HEAD_SIZE)
    head_gradients = output_gradient.reshape(query_tokens, KEY_VALUE_HEADS, group_width * HEAD_SIZE)
    query_parts, key_parts, value_parts = ([], [], [])
    for key_value_head in range(KEY_VALUE_HEADS):
        query_block = query_head_rows[:, key_value_head].reshape(
            query_tokens * group_width, HEAD_SIZE
        )
        out_block = output_heads[:, key_value_head].reshape(query_tokens * group_width, HEAD_SIZE)
        grad_block = head_gradients[:, key_value_head].reshape(
            query_tokens * group_width, HEAD_SIZE
        )
        key_block = key_tokens[:, key_value_head * HEAD_SIZE : (key_value_head + 1) * HEAD_SIZE]
        value_block = values[:, key_value_head * HEAD_SIZE : (key_value_head + 1) * HEAD_SIZE]
        scores = contract_cols(query_block, key_block) * score_scale
        scores = jnp.where(visible, scores, -1e30)
        row_max = jnp.max(scores, axis=1, keepdims=True)
        weights = jnp.exp(scores - row_max)
        attn_probs = weights / jnp.sum(weights, axis=1, keepdims=True)
        probs_b = attn_probs.astype(jnp.bfloat16)
        dprobs = contract_cols(grad_block, value_block)
        row_delta = jnp.sum(
            grad_block.astype(jnp.float32) * out_block.astype(jnp.float32), axis=1, keepdims=True
        )
        dscores = (attn_probs * (dprobs - row_delta)).astype(jnp.bfloat16)
        grad_query = jnp.dot(dscores, key_block, preferred_element_type=jnp.float32) * score_scale
        grad_key = contract_rows(dscores, query_block) * score_scale
        grad_value = contract_rows(probs_b, grad_block)
        query_parts.append(grad_query.reshape(query_tokens, group_width * HEAD_SIZE))
        key_parts.append(grad_key)
        value_parts.append(grad_value)
    query_grad = jnp.concatenate(query_parts, axis=1).astype(jnp.bfloat16)
    kv_partial = jnp.concatenate(key_parts + value_parts, axis=1).astype(jnp.bfloat16)
    return (query_grad, kv_partial)


def on_device(
    queries,
    branch_keys,
    branch_value_rows,
    attention_output,
    output_gradient,
    anc_states,
    key_matrix,
    value_matrix,
    anc_blocks,
    anc_count,
):
    key_value_width = key_matrix.shape[1]
    kv_weight = jnp.concatenate([key_matrix, value_matrix], axis=1)
    owned_blocks = anc_states.shape[0] // BLK
    own_kv = jnp.dot(anc_states, kv_weight, preferred_element_type=jnp.float32).astype(jnp.bfloat16)
    own_kv = own_kv.reshape(owned_blocks, BLK, 2 * key_value_width)
    block_ids = anc_blocks[0]
    slot_index = jnp.arange(NA, dtype=jnp.int32)
    live_slot = slot_index < anc_count[0]
    leaves = lax.axis_size("leaf")
    shard_kv = lax.all_gather(own_kv, "leaf", axis=0, tiled=True)
    blocks = shard_kv.shape[0]
    onehot = (
        (block_ids[:, None] == jnp.arange(blocks, dtype=jnp.int32)[None, :]) & live_slot[:, None]
    ).astype(jnp.bfloat16)
    found = jnp.einsum("ab,btf->atf", onehot, shard_kv, preferred_element_type=jnp.float32)
    slot_kv = found.astype(jnp.bfloat16)
    flat_kv = slot_kv.reshape(NA * BLK, 2 * key_value_width)
    key_tokens = jnp.concatenate([flat_kv[:, :key_value_width], branch_keys], axis=0)
    values = jnp.concatenate([flat_kv[:, key_value_width:], branch_value_rows], axis=0)
    key_live = jnp.concatenate(
        [jnp.repeat(live_slot, BLK), jnp.ones((queries.shape[0],), dtype=bool)]
    )
    query_grad, kv_partial = attend(
        queries, key_tokens, values, attention_output, output_gradient, key_live
    )
    branch_part = kv_partial[NA * BLK :]
    slot_grads = kv_partial[: NA * BLK].reshape(NA, BLK, 2 * key_value_width)
    blocks = lax.axis_size("leaf") * (owned_blocks * BLK) // BLK
    onehot = (
        (block_ids[None, :] == jnp.arange(blocks, dtype=jnp.int32)[:, None]) & live_slot[None, :]
    ).astype(jnp.bfloat16)
    found = jnp.einsum("ba,atf->btf", onehot, slot_grads, preferred_element_type=jnp.float32)
    totals = lax.psum_scatter(
        found.reshape(lax.axis_size("leaf") * (owned_blocks * BLK), 2 * key_value_width).astype(
            jnp.bfloat16
        ),
        "leaf",
        scatter_dimension=0,
        tiled=True,
    )
    anc_state_grad = contract_cols(totals, kv_weight).astype(jnp.bfloat16)
    shards = lax.axis_size("dp") * leaves
    weight_grad = lax.psum_scatter(
        contract_rows(anc_states, totals), ("dp", "leaf"), scatter_dimension=0, tiled=True
    )
    weight_grad = weight_grad / shards
    return (
        query_grad,
        branch_part[:, :key_value_width],
        branch_part[:, key_value_width:],
        anc_state_grad,
        weight_grad[:, :key_value_width],
        weight_grad[:, key_value_width:],
    )


def solution(mesh):
    return jax.shard_map(
        on_device,
        mesh=mesh,
        in_specs=(
            P(("dp", "leaf"), None),
            P(("dp", "leaf"), None),
            P(("dp", "leaf"), None),
            P(("dp", "leaf"), None),
            P(("dp", "leaf"), None),
            P(("dp", "leaf"), None),
            P(),
            P(),
            P(("dp", "leaf"), None),
            P(("dp", "leaf")),
        ),
        out_specs=(
            P(("dp", "leaf"), None),
            P(("dp", "leaf"), None),
            P(("dp", "leaf"), None),
            P(("dp", "leaf"), None),
            P(("dp", "leaf"), None),
            P(("dp", "leaf"), None),
        ),
        check_vma=False,
    )
```

profile of v0, /device:TPU:1, one launch (start us, length us, event | category | flops | bytes accessed | tf_op | source)
XLA Modules:
  0.0 486.0 jit_solution(6908011586716955942)
XLA Ops:
  7.2 2.6 constant_dynamic-update-slice_fusion.1
  11.0 2.5 convolution_convert_fusion.2
  15.0 3.3 reshape.107
  18.3 10.7 %slice_reduce_fusion.7 = (bf16[256,896]{1,0:T(8,128)(2,1)}, bf16[256,896]{1,0:T(8,128)(2,1)}, bf16[256,896]{1,0:T(8,128)(2,1)}, bf16[256,896]{1,0:T(8,128)(2,1)S(1)}) fusion(bf16[256,4,896]{2,1,0:T(4,128)(2,1)S(1)} %reshape.107), kind=kLoop, calls=%fused_computation.89 | loop fusion | bytes 3670016 | tf_op jit(solution)/shard_map/slice | solution.py:42
  29.0 2.2 reshape_squeeze.28
  31.3 2.2 reshape_squeeze.32
  33.5 2.3 reshape_squeeze.30
  37.0 3.3 reshape.109
  40.3 4.2 reshape.108
  44.6 14.3 %slice_reduce_fusion.6 = (bf16[256,896]{1,0:T(8,128)(2,1)}, bf16[256,896]{1,0:T(8,128)(2,1)}, bf16[256,896]{1,0:T(8,128)(2,1)S(1)}, bf16[256,896]{1,0:T(8,128)(2,1)}) fusion(bf16[256,4,896]{2,1,0:T(4,128)(2,1)} %reshape.108), kind=kLoop, calls=%fused_computation.88 | loop fusion | bytes 3670016 | tf_op jit(solution)/shard_map/slice | solution.py:46
  58.9 2.3 reshape_squeeze.29
  61.1 2.3 reshape_squeeze.33
  66.1 4.0 fusion.84
  71.6 2.2 reshape.116
  73.7 2.2 reshape.115
  84.8 12.4 %fusion.47 = bf16[16,64,1024]{2,0,1:T(8,128)(2,1)S(1)} fusion(bf16[64,64,1024]{2,1,0:T(8,128)(2,1)} %all-gather.2.cloned.1.call-done, s32[16]{0:T(128)S(1)} %bitcast.89, pred[16]{0:T(512)(128)(4,1)S(1)} %iota_compare_fusion.3), kind=kOutput, calls=%fused_computation.73 | convolution fusion | flops 135268352 | bytes 10485840 | tf_op jit(solution)/shard_map/ab,btf->atf/dot_general | solution.py:99
  98.7 2.6 fusion.89
  102.9 3.1 fusion.3
  107.7 6.1 %fusion.88 = (f32[1792]{0:T(1024)S(1)}, f32[1792,1280]{0,1:T(8,128)}) fusion(bf16[1792,128]{1,0:T(8,128)(2,1)S(1)} %copy-done.19, bf16[1024,512]{1,0:T(8,128)(2,1)S(1)} %get-tuple-element.33, bf16[256,512]{1,0:T(8,128)(2,1)S(1)} %copy-done.7, s32[1792]{0:T(1024)S(1)} %add_select_fusion, s32[1280]{0:T(1024)S(1)} %iota_add_fusion, ...), kind=kOutput, calls=%fused_computation.153 | convolution fusion | flops 599324928 | bytes 10966528 | tf_op jit(solution)/shard_map/dot_general | solution.py:22
  113.7 6.5 %fusion.87 = (f32[1792]{0:T(1024)S(1)}, f32[1792,1280]{0,1:T(8,128)}) fusion(bf16[1792,128]{1,0:T(8,128)(2,1)S(1)} %copy-done.15, bf16[1024,512]{1,0:T(8,128)(2,1)S(1)} %get-tuple-element.33, bf16[256,512]{1,0:T(8,128)(2,1)S(1)} %copy-done.7, s32[1792]{0:T(1024)S(1)} %add_select_fusion, s32[1280]{0:T(1024)S(1)} %iota_add_fusion, ...), kind=kOutput, calls=%fused_computation.152 | convolution fusion | flops 599324928 | bytes 10966528 | tf_op jit(solution)/shard_map/dot_general | solution.py:22
  120.3 2.6 fusion.86
  124.1 3.0 fusion
  127.2 6.5 %fusion.9 = f32[1792]{0:T(1024)S(1)} fusion(f32[1792,1280]{0,1:T(8,128)} %get-tuple-element.45, f32[1792]{0:T(1024)S(1)} %get-tuple-element.44), kind=kLoop, calls=%fused_computation.31 | loop fusion | flops 4585728 | bytes 9189376 | tf_op jit(solution)/shard_map/reduce_sum | solution.py:55
  133.8 5.2 %fusion.2 = bf16[1792,1280]{0,1:T(8,128)(2,1)S(1)} fusion(bf16[1792,128]{1,0:T(8,128)(2,1)S(1)} %copy-done.17, f32[1792]{0:T(1024)S(1)} %multiply_reduce_fusion.2, f32[1792]{0:T(1024)S(1)} %fusion.9, f32[1792,1280]{0,1:T(8,128)} %get-tuple-element.45, f32[1792]{0:T(1024)S(1)} %get-tuple-element.44, bf16[1024,512]{1,0:T(8,128)(2,1)S(1)} %get-tuple-element.32, ...), kind=kOutput, calls=%fused_computation.15 | convolution fusion | flops 599326720 | bytes 15553536 | tf_op jit(solution)/shard_map/dot_general | solution.py:22
  139.0 2.0 copy-done.4
  142.7 4.9 %fusion.11 = f32[1792]{0:T(1024)S(1)} fusion(f32[1792,1280]{0,1:T(8,128)} %get-tuple-element.43, f32[1792]{0:T(1024)S(1)} %get-tuple-element.42), kind=kLoop, calls=%fused_computation.33 | loop fusion | flops 4585728 | bytes 9189376 | tf_op jit(solution)/shard_map/reduce_sum | solution.py:55
  147.6 5.4 %fusion.1 = bf16[1792,1280]{0,1:T(8,128)(2,1)S(1)} fusion(bf16[1792,128]{1,0:T(8,128)(2,1)S(1)} %copy-done.14, f32[1792]{0:T(1024)S(1)} %multiply_reduce_fusion.1, f32[1792]{0:T(1024)S(1)} %fusion.11, f32[1792,1280]{0,1:T(8,128)} %get-tuple-element.43, f32[1792]{0:T(1024)S(1)} %get-tuple-element.42, bf16[1024,512]{1,0:T(8,128)(2,1)S(1)} %get-tuple-element.32, ...), kind=kOutput, calls=%fused_computation.12 | convolution fusion | flops 599326720 | bytes 15553536 | tf_op jit(solution)/shard_map/dot_general | solution.py:22
  156.3 6.4 %constant_dynamic-update-slice_fusion.5 = (bf16[1280,1024]{0,1:T(8,128)(2,1)S(1)}, bf16[1280,128]{0,1:T(8,128)(2,1)}) fusion(bf16[1280,1024]{0,1:T(8,128)(2,1)S(1)} %get-tuple-element.54, bf16[1792,128]{1,0:T(8,128)(2,1)S(1)} %copy-done.18, f32[1792]{0:T(1024)S(1)} %fusion.7, f32[1792,1280]{0,1:T(8,128)} %copy-done.6, f32[1792]{0:T(1024)S(1)} %get-tuple-element.46), kind=kOutput, calls=%fused_computation.119 | convolution fusion | flops 594247680 | bytes 10305536 | tf_op jit(solution)/shard_map/dot_general | solution.py:16
  162.8 6.3 %constant_dynamic-update-slice_fusion.4 = (bf16[1280,1024]{0,1:T(8,128)(2,1)S(1)}, bf16[1280,128]{0,1:T(8,128)(2,1)}) fusion(bf16[1280,1024]{0,1:T(8,128)(2,1)S(1)} %get-tuple-element.56, bf16[1792,128]{1,0:T(8,128)(2,1)S(1)} %copy-done.17, f32[1792]{0:T(1024)S(1)} %fusion.9, f32[1792,1280]{0,1:T(8,128)} %get-tuple-element.45, f32[1792]{0:T(1024)S(1)} %get-tuple-element.44), kind=kOutput, calls=%fused_computation.118 | convolution fusion | flops 594247680 | bytes 10305536 | tf_op jit(solution)/shard_map/dot_general | solution.py:16
  169.1 2.7 constant_dynamic-update-slice_fusion.3
  171.8 2.6 constant_dynamic-update-slice_fusion.2
  176.1 3.9 copy.57
  180.0 7.3 %convolution_convert_fusion = bf16[64,64,1024]{2,0,1:T(8,128)(2,1)} fusion(bf16[16,64,1024]{2,1,0:T(8,128)(2,1)} %bitcast.87, s32[16]{0:T(128)S(1)} %bitcast.90, pred[16]{0:T(512)(128)(4,1)S(1)} %iota_compare_fusion.3), kind=kOutput, calls=%fused_computation.36 | convolution fusion | flops 138414080 | bytes 10485840 | tf_op jit(solution)/shard_map/ba,atf->btf/dot_general | solution.py:116
  187.3 11.3 %copy.59 = bf16[64,64,1024]{2,1,0:T(8,128)(2,1)} copy(bf16[64,64,1024]{2,0,1:T(8,128)(2,1)} %convolution_convert_fusion) | data formatting | bytes 16777216 | tf_op jit(solution)/shard_map/convert_element_type | solution.py:118
  198.9 94.4 %reduce-scatter.3.cloned.1.call-done = bf16[128,1024]{1,0:T(8,128)(2,1)} async-done(((bf16[4096,1024]{1,0:T(8,128)(2,1)}), bf16[128,1024]{1,0:T(8,128)(2,1)}) %reduce-scatter.3.cloned.1.call-update) | async-done | bytes 262160 | tf_op jit(solution)/shard_map/reduce_scatter | solution.py:117
  293.2 8.2 %convolution_bitcast_fusion = f32[3584,1024]{0,1:T(8,128)} fusion(bf16[128,1024]{1,0:T(8,128)(2,1)} %reduce-scatter.3.cloned.1.call-done, bf16[128,3584]{1,0:T(8,128)(2,1)S(1)} %copy-done), kind=kOutput, calls=%fused_computation.25 | convolution fusion | flops 939524096 | bytes 15859712 | tf_op jit(solution)/shard_map/dot_general | solution.py:16
  301.5 4.5 fusion.41
  306.0 2.3 reshape.113
  308.3 4.5 fusion.38
  312.8 2.3 reshape.110
  315.0 4.8 fusion.39
  319.8 2.3 reshape.111
  323.8 1.8 copy.61
  326.3 1.9 copy.60
  328.2 3.8 fusion.40
  332.5 2.5 pad_maximum_fusion
  335.1 6.8 %convolution_convert_fusion.1 = bf16[128,3584]{1,0:T(8,128)(2,1)} fusion(bf16[128,1024]{1,0:T(8,128)(2,1)S(1)} %copy-done.21, bf16[3584,1024]{1,0:T(8,128)(2,1)} %copy-done.1), kind=kOutput, calls=%fused_computation.37 | convolution fusion | flops 939982848 | bytes 8519680 | tf_op jit(solution)/shard_map/dot_general | solution.py:22
  341.9 134.3 %all-reduce.4.cloned.1.call-done = f32[3584,1024]{0,1:T(8,128)} async-done(((f32[3584,1024]{0,1:T(8,128)}), f32[3584,1024]{0,1:T(8,128)}) %all-reduce.4.cloned.1.call-update) | async-done | bytes 14680080
  (99 shorter events, 35.0 us)
Async XLA Ops:
  7.2 3.9 copy-start
  7.2 77.6 %all-gather.2.cloned.1.call-start = ((), (), s32[]{:S(2)}) async-start(), calls=%async_computation.1 | async-start | bytes 8650752 | tf_op jit(solution)/shard_map/all_gather | solution.py:94
  7.2 3.2 copy-start.10
  11.0 3.1 copy-start.1
  14.1 279.1 %reduce-scatter.3.cloned.1.call-start = ((), (), s32[]{:S(2)}) async-start(), calls=%async_computation.2 | async-start | bytes 8650752 | tf_op jit(solution)/shard_map/reduce_scatter | solution.py:117
  66.1 58.0 %copy-start.12 = (bf16[1792,128]{1,0:T(8,128)(2,1)}, bf16[1792,128]{1,0:T(8,128)(2,1)S(1)}, u32[]{:S(2)}) copy-start(bf16[1792,128]{1,0:T(8,128)(2,1)S(1)} %reshape_squeeze.35) | copy-start | bytes 1376260
  70.1 5.8 %copy-start.8 = (bf16[256,1,896]{2,1,0:T(2,128)(2,1)S(1)}, bf16[256,1,896]{2,1,0:T(2,128)(2,1)}, u32[]{:S(2)}) copy-start(bf16[256,1,896]{2,1,0:T(2,128)(2,1)} %get-tuple-element.35) | copy-start | bytes 1376260
  70.1 5.8 %copy-start.9 = (bf16[256,1,896]{2,1,0:T(2,128)(2,1)S(1)}, bf16[256,1,896]{2,1,0:T(2,128)(2,1)}, u32[]{:S(2)}) copy-start(bf16[256,1,896]{2,1,0:T(2,128)(2,1)} %get-tuple-element.37) | copy-start | bytes 1376260
  73.7 11.0 %copy-start.23 = (s32[1,16]{1,0:T(1,128)S(1)}, s32[1,16]{1,0:T(1,128)}, u32[]{:S(2)}) copy-start(s32[1,16]{1,0:T(1,128)} %param.18) | copy-start | bytes 196
  84.8 13.8 %copy-start.7 = (bf16[256,512]{1,0:T(8,128)(2,1)S(1)}, bf16[256,512]{1,0:T(8,128)(2,1)}, u32[]{:S(2)}) copy-start(bf16[256,512]{1,0:T(8,128)(2,1)} %param.11) | copy-start | bytes 786436
  97.1 1.5 copy-start.20
  98.7 21.6 %copy-start.22 = (bf16[1280,128]{1,0:T(8,128)(2,1)}, bf16[1280,128]{1,0:T(8,128)(2,1)S(1)}, u32[]{:S(2)}) copy-start(bf16[1280,128]{1,0:T(8,128)(2,1)S(1)} %pad_maximum_fusion.3) | copy-start | bytes 983044
  101.2 4.7 copy-start.6
  101.3 1.4 copy-start.18
  101.3 1.6 copy-start.24
  106.0 7.8 %copy-start.2 = (bf16[1792,1280]{0,1:T(8,128)(2,1)}, bf16[1792,1280]{0,1:T(8,128)(2,1)S(1)}, u32[]{:S(2)}) copy-start(bf16[1792,1280]{0,1:T(8,128)(2,1)S(1)} %fusion.3) | copy-start | bytes 13762564
  106.0 1.7 copy-start.19
  107.7 6.1 %copy-start.15 = (bf16[1792,128]{1,0:T(8,128)(2,1)S(1)}, bf16[1792,128]{1,0:T(8,128)(2,1)}, u32[]{:S(2)}) copy-start(bf16[1792,128]{1,0:T(8,128)(2,1)} %reshape_squeeze.32) | copy-start | bytes 1376260
  113.7 6.5 %copy-start.16 = (bf16[1792,128]{1,0:T(8,128)(2,1)S(1)}, bf16[1792,128]{1,0:T(8,128)(2,1)}, u32[]{:S(2)}) copy-start(bf16[1792,128]{1,0:T(8,128)(2,1)} %reshape_squeeze.34) | copy-start | bytes 1376260
  127.2 27.4 %copy-start.5 = (bf16[1792,1280]{0,1:T(8,128)(2,1)}, bf16[1792,1280]{0,1:T(8,128)(2,1)S(1)}, u32[]{:S(2)}) copy-start(bf16[1792,1280]{0,1:T(8,128)(2,1)S(1)} %fusion) | copy-start | bytes 13762564
  127.2 6.6 %copy-start.17 = (bf16[1792,128]{1,0:T(8,128)(2,1)S(1)}, bf16[1792,128]{1,0:T(8,128)(2,1)}, u32[]{:S(2)}) copy-start(bf16[1792,128]{1,0:T(8,128)(2,1)} %reshape_squeeze.31) | copy-start | bytes 1376260
  139.0 2.1 copy-start.4
  141.0 6.6 %copy-start.14 = (bf16[1792,128]{1,0:T(8,128)(2,1)S(1)}, bf16[1792,128]{1,0:T(8,128)(2,1)}, u32[]{:S(2)}) copy-start(bf16[1792,128]{1,0:T(8,128)(2,1)} %reshape_squeeze.33) | copy-start | bytes 1376260
  153.0 3.4 copy-start.3
  156.3 12.8 %slice-start = ((s8[9175040]{0:T(1024)(128)(4,1)}), s8[4194304]{0:T(1024)(128)(4,1)S(1)}, s32[]{:S(2)}) async-start(s8[9175040]{0:T(1024)(128)(4,1)} %bitcast.84), calls=%async_computation.4 | async-start | bytes 8388608
  156.3 12.8 %slice-start.1 = ((s8[9175040]{0:T(1024)(128)(4,1)}), s8[4194304]{0:T(1024)(128)(4,1)S(1)}, s32[]{:S(2)}) async-start(s8[9175040]{0:T(1024)(128)(4,1)} %bitcast.84), calls=%async_computation.5 | async-start | bytes 8388608
  162.7 6.4 %slice-start.2 = ((s8[9175040]{0:T(1024)(128)(4,1)}), s8[786432]{0:T(1024)(128)(4,1)S(1)}, s32[]{:S(2)}) async-start(s8[9175040]{0:T(1024)(128)(4,1)} %bitcast.84), calls=%async_computation.6 | async-start | bytes 1572864
  169.1 2.7 copy-start.13
  198.6 277.6 %all-reduce.4.cloned.1.call-start = ((), (), s32[]{:S(2)}) async-start(), calls=%async_computation.3 | async-start | bytes 29360128
  326.3 6.2 %copy-start.11 = (bf16[256,896]{1,0:T(8,128)(2,1)S(1)}, bf16[256,896]{1,0:T(8,128)(2,1)}, u32[]{:S(2)}) copy-start(bf16[256,896]{1,0:T(8,128)(2,1)} %reshape.113) | copy-start | bytes 1376260
  326.3 8.8 %copy-start.21 = (bf16[128,1024]{1,0:T(8,128)(2,1)S(1)}, bf16[128,1024]{1,0:T(8,128)(2,1)}, u32[]{:S(2)}) copy-start(bf16[128,1024]{1,0:T(8,128)(2,1)} %reduce-scatter.3.cloned.1.call-done) | copy-start | bytes 786436
Sparse Core Ops, SparseCore 0:
  14.3 56.6 all-gather.1
  198.7 94.4 reduce-scatter.2
  301.6 174.5 all-reduce.3
where the time goes:
time: 495 us; the launch traced here: 486 us
  waiting for transfers between devices  229 us (46%)
  matrix products  114 us (23%)
  local copies, waits for them, and re-layouts  99.7 us (20%)
  other arithmetic  28.1 us (6%)
  between operations  15.3 us (3%)
    unnamed x4, waiting for transfers between devices  134 us
    reduce_scatter x1, waiting for transfers between devices, on_device(): lax.psum_scatter(found.reshape(lax.axis_size('leaf') * (owned_blocks * BL...  94.4 us
    dot_general x9, matrix products, contract_cols(): lax.dot_general(left, right, (((1,), (1,)), ((), ())), preferred_element_...  41.2 us
    dot_general x9, matrix products, contract_rows(): lax.dot_general(left, right, (((0,), (0,)), ((), ())), preferred_element_...  33 us
    dot_general x4, matrix products, attend(): jnp.dot(dscores, key_block, preferred_element_type=jnp.float32)  17.6 us
    slice x1, local copies, waits for them, and re-layouts, attend(): head_gradients[:, key_value_head]  14.3 us
    reduce_sum x4, other arithmetic, attend(): attn_probs = weights / jnp.sum(weights, axis=1, keepdims=True)  14 us
    dot_general x1, matrix products, on_device(): jnp.einsum('ab,btf->atf', onehot, shard_kv, preferred_element_type=jnp.fl...  12.4 us
  transfers between devices with their start and end apart: 3, of which 2 were waited for; matrix products, arithmetic and copies ran while one was open for 23% of the time, Pallas kernels for 0%

commit v1 on v0

v1 whole, which is shorter than its diff:
```python
import functools
import math

import jax
import jax.numpy as jnp
from jax import lax
from jax.experimental import pallas as pl
from jax.experimental.pallas import tpu as pltpu
from jax.sharding import PartitionSpec as P

BF = jnp.bfloat16
F32 = jnp.float32
WIDTH = 3584
HEADS = 4
GROUP = 7
HEAD = 128
NA = 16
BLK = 64
TOK = 256
ANC = NA * BLK
KEYS = ANC + TOK
OWN = 128
COLS = WIDTH // 4
SCALE = 1.0 / math.sqrt(HEAD)
EXP2_SCALE = SCALE * math.log2(math.e)
NEG = -1e30
MIB = 1024 * 1024


def contract_rows(left, right):
    return lax.dot_general(left, right, (((0,), (0,)), ((), ())), preferred_element_type=F32)


def contract_cols(left, right):
    return lax.dot_general(left, right, (((1,), (1,)), ((), ())), preferred_element_type=F32)


def wrap(v):
    return lax.rem(v + 4, 4)


class Place:
    def __init__(self):
        leaf = lax.axis_index("leaf")
        self.g = lax.axis_index("dp")
        self.leaf = leaf
        self.c = lax.rem(leaf, 2)
        y = lax.rem(lax.div(leaf, 2), 4)
        z = lax.div(leaf, 8)
        self.a = z + self.c * (y - z)
        self.b = y + self.c * (z - y)

    def chip(self, a, b):
        return a * 4 + b + self.c * (3 * b - 3 * a)

    def at(self, a, b):
        return (self.g, self.chip(a, b) * 2 + self.c)

    def sibling(self):
        return (self.g, self.leaf + 1 - 2 * self.c)

    def along_x(self, d):
        return (wrap(self.g + d), self.leaf)

    def ring(self):
        return {
            "b+": self.at(self.a, wrap(self.b + 1)),
            "b-": self.at(self.a, wrap(self.b - 1)),
            "a+": self.at(wrap(self.a + 1), self.b),
            "a-": self.at(wrap(self.a - 1), self.b),
        }


def send(src, dst, ssem, rsem, to):
    copy = pltpu.make_async_remote_copy(
        src_ref=src,
        dst_ref=dst,
        send_sem=ssem,
        recv_sem=rsem,
        device_id=to,
        device_id_type=pl.DeviceIdType.MESH,
    )
    copy.start()
    return copy


def greet(me):
    barrier = pltpu.get_barrier_semaphore()
    others = list(me.ring().values()) + [me.sibling()] + [me.along_x(d) for d in (1, 2, 3)]
    for other in others:
        pl.semaphore_signal(barrier, inc=1, device_id=other, device_id_type=pl.DeviceIdType.MESH)
    pl.semaphore_wait(barrier, len(others))


def gather_kernel(
    anc_hbm, wk_hbm, wv_hbm, kvg_out, ancx_out,
    anc, wk, wv, own, kvg0, kvg1, kvg2, kvg3, ancx, lsem, osem, ssem, rsem, xssem, xrsem,
):
    me = Place()
    c, a, b = me.c, me.a, me.b
    kvg = [kvg0, kvg1, kvg2, kvg3]
    loads = [
        pltpu.make_async_copy(anc_hbm, anc, lsem.at[0]),
        pltpu.make_async_copy(wk_hbm, wk, lsem.at[1]),
        pltpu.make_async_copy(wv_hbm, wv, lsem.at[2]),
    ]
    for load in loads:
        load.start()
    greet(me)
    ring = me.ring()
    ab, bb = wrap(a + 1), wrap(a - 1)
    sib = me.sibling()
    away = []
    for d in (1, 2, 3):
        cols = pl.ds(pl.multiple_of(wrap(me.g + d) * COLS, 128), COLS)
        away.append(
            send(anc_hbm.at[:, cols], ancx.at[me.g, c], xssem.at[d], xrsem.at[d], me.along_x(d))
        )
    loads[0].wait()
    mine = pl.ds(pl.multiple_of(me.g * COLS, 128), COLS)
    ancx[me.g, c] = anc[:, mine]
    for t, (w, load) in enumerate(((wk, loads[1]), (wv, loads[2]))):
        load.wait()
        kv = jnp.dot(anc[...], w[...], preferred_element_type=F32).astype(BF)
        for h in range(HEADS):
            own[t, h] = kv[:, h * HEAD : (h + 1) * HEAD]
    copies = [{} for _ in range(HEADS)]

    def go(h, k, src, dst, to):
        copies[h][k] = send(src, dst, ssem.at[h, k], rsem.at[h, k], to)

    for h in range(HEADS):
        go(h, 0, own.at[1 - c, h], kvg[h].at[1 - c, b, a, c], sib)
        kvg[h][c, a, b, c] = own[c, h]
    for h in range(HEADS):
        copies[h][0].wait_recv()
        here = kvg[h].at[c, a, b]
        go(h, 1, here, here, ring["b+"])
        go(h, 2, here, here, ring["b-"])
    for h in range(HEADS):
        copies[h][1].wait_recv()
        half = kvg[h].at[c, a, wrap(b - 1), 0]
        go(h, 3, half, half, ring["b+"])
        copies[h][2].wait_recv()
        half = kvg[h].at[c, a, wrap(b + 1), 1]
        go(h, 4, half, half, ring["b-"])
    for h in range(HEADS):
        copies[h][3].wait_recv()
        copies[h][4].wait_recv()
        row = kvg[h].at[c, a]
        go(h, 5, row, row, ring["a+"])
        go(h, 6, row, row, ring["a-"])
        go(h, 9, row, row, sib)
    sent_x = []
    sent_x.append(send(ancx.at[me.g, c], ancx.at[me.g, c], xssem.at[4], xrsem.at[4], sib))
    for d in (1, 2, 3):
        away[d - 1].wait_recv()
        part = ancx.at[wrap(me.g - d), c]
        sent_x.append(send(part, part, xssem.at[4 + d], xrsem.at[4 + d], sib))
    for h in range(HEADS):
        copies[h][5].wait_recv()
        half = kvg[h].at[c, wrap(a - 1), pl.ds(0, 2)]
        go(h, 7, half, half, ring["a+"])
        row = kvg[h].at[c, wrap(a - 1)]
        go(h, 10, row, row, sib)
        copies[h][6].wait_recv()
        half = kvg[h].at[c, wrap(a + 1), pl.ds(2, 2)]
        go(h, 8, half, half, ring["a-"])
        row = kvg[h].at[c, wrap(a + 1)]
        go(h, 11, row, row, sib)
    for h in range(HEADS):
        copies[h][7].wait_recv()
        copies[h][8].wait_recv()
        row = kvg[h].at[c, wrap(a + 2)]
        go(h, 12, row, row, sib)
    for copy in sent_x:
        copy.wait_recv()
    outs = [pltpu.make_async_copy(ancx, ancx_out, osem.at[HEADS])]
    outs[0].start()
    for h in range(HEADS):
        for k in (9, 10, 11, 12):
            copies[h][k].wait_recv()
        out = pltpu.make_async_copy(kvg[h], kvg_out.at[h], osem.at[h])
        out.start()
        outs.append(out)
    for h in range(HEADS):
        for k in range(13):
            copies[h][k].wait_send()
    for copy in away + sent_x:
        copy.wait_send()
    for out in outs:
        out.wait()


def gather_call(anc, wk, wv):
    hbm = pl.BlockSpec(memory_space=pl.ANY)
    kvg = pltpu.VMEM((2, 4, 4, 2, OWN, HEAD), BF)
    return pl.pallas_call(
        gather_kernel,
        out_shape=(
            jax.ShapeDtypeStruct((HEADS, 2, 4, 4, 2, OWN, HEAD), BF),
            jax.ShapeDtypeStruct((4, 2, OWN, COLS), BF),
        ),
        in_specs=[hbm] * 3,
        out_specs=(hbm, hbm),
        scratch_shapes=[
            pltpu.VMEM((OWN, WIDTH), BF),
            pltpu.VMEM((WIDTH, HEADS * HEAD), BF),
            pltpu.VMEM((WIDTH, HEADS * HEAD), BF),
            pltpu.VMEM((2, HEADS, OWN, HEAD), BF),
            kvg, kvg, kvg, kvg,
            pltpu.VMEM((4, 2, OWN, COLS), BF),
            pltpu.SemaphoreType.DMA((3,)),
            pltpu.SemaphoreType.DMA((HEADS + 1,)),
            pltpu.SemaphoreType.DMA((HEADS, 13)),
            pltpu.SemaphoreType.DMA((HEADS, 13)),
            pltpu.SemaphoreType.DMA((8,)),
            pltpu.SemaphoreType.DMA((8,)),
        ],
        compiler_params=pltpu.CompilerParams(
            collective_id=0, has_side_effects=True, vmem_limit_bytes=56 * MIB
        ),
        name="gather_kv",
    )(anc, wk, wv)


def attend_kernel(
    blocks, count, kvg, q, out, grad, bk, bv, dq_out, slots_out, dbk_out, dbv_out,
    ks, vs, kt, s, dk, dv,
):
    for j in range(NA):
        blk = blocks[0, j]
        leaf = lax.div(blk, 2)
        z, y, d = lax.div(leaf, 8), lax.rem(lax.div(leaf, 2), 4), lax.rem(leaf, 2)
        part = lax.rem(blk, 2)
        rows = pl.ds(j * BLK, BLK)
        ks[rows] = kvg[0, 0, ((z * 4 + y) * 2 + d) * 2 + part]
        vs[rows] = kvg[0, 1, ((y * 4 + z) * 2 + d) * 2 + part]
    ks[pl.ds(ANC, TOK)] = bk[...]
    vs[pl.ds(ANC, TOK)] = bv[...]
    kt[...] = ks[...].T
    dk[...] = jnp.zeros_like(dk)
    dv[...] = jnp.zeros_like(dv)
    live = [j < count[0] for j in range(NA)]
    ones = jnp.ones((8, HEAD), BF)

    def one(h, carry):
        cols = pl.ds(pl.multiple_of(h * HEAD, HEAD), HEAD)
        qh = q[:, cols]
        gh = grad[:, cols]
        prod = gh.astype(F32) * out[:, cols].astype(F32)
        hi = prod.astype(BF)
        lo = (prod - hi.astype(F32)).astype(BF)
        delta = (contract_cols(ones, hi) + contract_cols(ones, lo))[0:1]
        top = jnp.full((8, TOK), NEG, F32)
        for ch in range(4):
            sc = contract_cols(ks[pl.ds(ch * 256, 256)], qh)
            s[pl.ds(ch * 256, 256)] = sc
            for j in range(4):
                part = sc[j * BLK : (j + 1) * BLK].reshape(8, 8, TOK).max(axis=0)
                top = jnp.maximum(top, jnp.where(live[ch * 4 + j], part, NEG))
        sc = contract_cols(ks[pl.ds(ANC, TOK)], qh)
        seen = lax.broadcasted_iota(jnp.int32, (TOK, TOK), 0) <= lax.broadcasted_iota(
            jnp.int32, (TOK, TOK), 1
        )
        sc = jnp.where(seen, sc, NEG)
        s[pl.ds(ANC, TOK)] = sc
        top = jnp.maximum(top, sc.reshape(32, 8, TOK).max(axis=0))
        top = top.max(axis=0, keepdims=True) * EXP2_SCALE
        total = jnp.zeros((8, TOK), F32)
        for j in range(NA):
            rows = pl.ds(j * BLK, BLK)
            e = jnp.exp2(s[rows] * EXP2_SCALE - jnp.where(live[j], top, 1e30))
            s[rows] = e
            total = total + e.reshape(8, 8, TOK).sum(axis=0)
        rows = pl.ds(ANC, TOK)
        e = jnp.exp2(s[rows] * EXP2_SCALE - top)
        s[rows] = e
        total = total + e.reshape(32, 8, TOK).sum(axis=0)
        inv = 1.0 / total.sum(axis=0, keepdims=True)
        dqt = jnp.zeros((HEAD, TOK), F32)
        for ch in range(5):
            rows = pl.ds(ch * 256, 256)
            p = s[rows] * inv
            dp = contract_cols(vs[rows], gh)
            ds = (p * (dp - delta)).astype(BF)
            dv[rows] += jnp.dot(p.astype(BF), gh, preferred_element_type=F32)
            dk[rows] += jnp.dot(ds, qh, preferred_element_type=F32)
            dqt = dqt + jnp.dot(kt[:, ch * 256 : (ch + 1) * 256], ds, preferred_element_type=F32)
        dq_out[:, cols] = (dqt * SCALE).T.astype(BF)
        return carry

    lax.fori_loop(0, GROUP, one, 0)
    slots_out[0, 0] = (dk[pl.ds(0, ANC)] * SCALE).astype(BF)
    slots_out[0, 1] = dv[pl.ds(0, ANC)].astype(BF)
    dbk_out[...] = (dk[pl.ds(ANC, TOK)] * SCALE).astype(BF)
    dbv_out[...] = dv[pl.ds(ANC, TOK)].astype(BF)


def attend_call(blocks, count, kvg, q, out, grad, bk, bv):
    smem = pl.BlockSpec(memory_space=pltpu.SMEM)
    wide = pl.BlockSpec((TOK, GROUP * HEAD), lambda h: (0, h))
    narrow = pl.BlockSpec((TOK, HEAD), lambda h: (0, h))
    return pl.pallas_call(
        attend_kernel,
        grid=(HEADS,),
        out_shape=(
            jax.ShapeDtypeStruct((TOK, WIDTH), BF),
            jax.ShapeDtypeStruct((HEADS, 2, ANC, HEAD), BF),
            jax.ShapeDtypeStruct((TOK, HEADS * HEAD), BF),
            jax.ShapeDtypeStruct((TOK, HEADS * HEAD), BF),
        ),
        in_specs=[
            smem,
            smem,
            pl.BlockSpec((1, 2, 64, BLK, HEAD), lambda h: (h, 0, 0, 0, 0)),
            wide,
            wide,
            wide,
            narrow,
            narrow,
        ],
        out_specs=(
            wide,
            pl.BlockSpec((1, 2, ANC, HEAD), lambda h: (h, 0, 0, 0)),
            narrow,
            narrow,
        ),
        scratch_shapes=[
            pltpu.VMEM((KEYS, HEAD), BF),
            pltpu.VMEM((KEYS, HEAD), BF),
            pltpu.VMEM((HEAD, KEYS), BF),
            pltpu.VMEM((KEYS, TOK), F32),
            pltpu.VMEM((KEYS, HEAD), F32),
            pltpu.VMEM((KEYS, HEAD), F32),
        ],
        compiler_params=pltpu.CompilerParams(vmem_limit_bytes=48 * MIB),
        name="attend",
    )(blocks, count, kvg.reshape(HEADS, 2, 64, BLK, HEAD), q, out, grad, bk, bv)


def add(x, y):
    return (x.astype(F32) + y.astype(F32)).astype(BF)


class Scatter:
    def __init__(self, me, data, first, full, edge, edge_first, edge_full, ssem, rsem):
        self.me, self.data, self.first, self.full = me, data, first, full
        self.edge, self.edge_first, self.edge_full = edge, edge_first, edge_full
        self.ssem, self.rsem = ssem, rsem
        self.copies = {}

    def go(self, k, src, dst, to):
        self.copies[k] = send(src, dst, self.ssem(k), self.rsem(k), self.me.ring()[to])

    def step(self, n):
        me, data = self.me, self.data
        up, down, far = wrap(me.a + 1), wrap(me.a - 1), wrap(me.a + 2)
        right, left, off = wrap(me.b + 1), wrap(me.b - 1), wrap(me.b + 2)
        copies = self.copies
        if n == 0:
            self.go(0, data.at[far, pl.ds(0, 2)], self.first.at[0], "a+")
            self.go(1, data.at[far, pl.ds(2, 2)], self.first.at[1], "a-")
        elif n == 1:
            copies[0].wait_recv()
            data[up, pl.ds(0, 2)] = add(data[up, pl.ds(0, 2)], self.first[0])
            self.go(2, data.at[up], self.full.at[0], "a+")
            copies[1].wait_recv()
            data[down, pl.ds(2, 2)] = add(data[down, pl.ds(2, 2)], self.first[1])
            self.go(3, data.at[down], self.full.at[1], "a-")
        elif n == 2:
            copies[2].wait_recv()
            copies[3].wait_recv()
            for j in range(4):
                b = wrap(me.b + (2, 1, 3, 0)[j])
                total = data[me.a, b].astype(F32) + self.full[0, b].astype(F32)
                self.edge[b] = (total + self.full[1, b].astype(F32)).astype(BF)
                if j == 0:
                    self.go(4, self.edge.at[off, 0], self.edge_first.at[0], "b+")
                    self.go(5, self.edge.at[off, 1], self.edge_first.at[1], "b-")
        elif n == 3:
            copies[4].wait_recv()
            self.edge[right, 0] = add(self.edge[right, 0], self.edge_first[0])
            self.go(6, self.edge.at[right], self.edge_full.at[0], "b+")
            copies[5].wait_recv()
            self.edge[left, 1] = add(self.edge[left, 1], self.edge_first[1])
            self.go(7, self.edge.at[left], self.edge_full.at[1], "b-")
        else:
            copies[6].wait_recv()
            copies[7].wait_recv()
            total = self.edge[me.b].astype(F32) + self.edge_full[0].astype(F32)
            return total + self.edge_full[1].astype(F32)

    def finish(self):
        for copy in self.copies.values():
            copy.wait_send()


def reduce_kernel(
    own_code, sib_code, slots, ancx, wk_hbm, wv_hbm, dstate_out, gk_out, gv_out,
    wk, wv, sib0, sib1, sib2, sib3, dense, first, full, edge, edge_first, edge_full,
    tot, pair, xt0, xt1, xt2, xt3, part, part_bf, wfirst, wfull, wedge, wedge_first, wedge_full,
    fin, fin_in, lsem, sibs, sibr, rss, rsr, prs, prr, xs, xr, ws, wr, fs, fr,
):
    me = Place()
    c = me.c
    sib = [sib0, sib1, sib2, sib3]
    xt = [xt0, xt1, xt2, xt3]
    loads = [
        pltpu.make_async_copy(wk_hbm, wk, lsem.at[0]),
        pltpu.make_async_copy(wv_hbm, wv, lsem.at[1]),
    ]
    for load in loads:
        load.start()
    greet(me)
    over = [send(slots.at[h, 1 - c], sib[h], sibs.at[h], sibr.at[h], me.sibling()) for h in range(HEADS)]
    runs = []
    for h in range(HEADS):
        run = Scatter(
            me, dense.at[h], first.at[h], full.at[h], edge.at[h], edge_first.at[h], edge_full.at[h],
            functools.partial(lambda h, k: rss.at[h, k], h),
            functools.partial(lambda h, k: rsr.at[h, k], h),
        )
        over[h].wait_recv()
        for i in (2, 1, 3, 0):
            row = wrap(me.a + i)
            for j in range(4):
                for d in range(2):
                    o = me.chip(row, j) * 2 + d
                    mine, theirs = own_code[o], sib_code[o]
                    slot = lax.div(mine, 4)
                    x = slots[h, c, slot]
                    slot = lax.div(theirs, 4)
                    y = sib[h][slot]
                    for block in range(2):
                        dense[h, row, j, d, pl.ds(block * BLK, BLK)] = add(
                            jnp.where(lax.rem(mine, 4) == block + 1, x, 0),
                            jnp.where(lax.rem(theirs, 4) == block + 1, y, 0),
                        )
            if i == 2:
                run.step(0)
        runs.append(run)
    for h in range(HEADS):
        runs[h].step(1)
    for h in range(HEADS):
        runs[h].step(2)
    for h in range(HEADS):
        runs[h].step(3)
    pairs, across, passed = [], [], []
    for h in range(HEADS):
        total = runs[h].step(4).astype(BF)
        tot[h] = total
        xt[h][me.g] = total
        pairs.append(send(tot.at[h, 1 - c], pair.at[h], prs.at[h], prr.at[h], me.sibling()))
        here = xt[h].at[me.g]
        across.append(
            [
                send(tot.at[h], here, xs.at[h, 0], xr.at[h, 0], me.along_x(1)),
                send(tot.at[h], here, xs.at[h, 1], xr.at[h, 1], me.along_x(-1)),
            ]
        )
    for h in range(HEADS):
        across[h][0].wait_recv()
        half = xt[h].at[wrap(me.g - 1), 0]
        passed.append(send(half, half, xs.at[h, 2], xr.at[h, 2], me.along_x(1)))
        across[h][1].wait_recv()
        half = xt[h].at[wrap(me.g + 1), 1]
        passed.append(send(half, half, xs.at[h, 3], xr.at[h, 3], me.along_x(-1)))
    for load in loads:
        load.wait()
    for h in range(HEADS):
        pairs[h].wait_recv()
    first_cols, last_cols = [], []
    for h in range(HEADS):
        mine, other = tot[h, c], pair[h]
        first_cols.append(jnp.where(c == 0, mine, other))
        last_cols.append(jnp.where(c == 0, other, mine))
    first_cols = jnp.concatenate(first_cols, axis=1)
    last_cols = jnp.concatenate(last_cols, axis=1)
    for n in range(0, WIDTH, 512):
        grad = contract_cols(first_cols, wk[pl.ds(n, 512)])
        grad = grad + contract_cols(last_cols, wv[pl.ds(n, 512)])
        dstate_out[:, pl.ds(n, 512)] = grad.astype(BF)
    for copy in passed:
        copy.wait_recv()
    totals = jnp.concatenate([xt[h][...].reshape(1024, HEAD) for h in range(HEADS)], axis=1)
    part[...] = contract_rows(ancx[...].reshape(1024, COLS), totals).reshape(16, 56, 512)
    run = Scatter(
        me, part_bf, wfirst, wfull, wedge, wedge_first, wedge_full,
        lambda k: ws.at[k], lambda k: wr.at[k],
    )
    for i in (2, 1, 3, 0):
        row = wrap(me.a + i)
        for j in range(4):
            x = part[me.chip(row, j)]
            x = jnp.concatenate([x, jnp.zeros((8, 512), F32)], axis=0).astype(BF)
            part_bf[row, j, 0] = x[:, :256]
            part_bf[row, j, 1] = x[:, 256:]
        if i == 2:
            run.step(0)
    for n in (1, 2, 3):
        run.step(n)
    done = run.step(4) * (1.0 / 128.0)
    fin[...] = done
    last = send(fin, fin_in, fs.at[0], fr.at[0], me.sibling())

    def rows_of(ref):
        both = jnp.concatenate([ref[0], ref[1]], axis=1)
        return jnp.where(c == 0, both[0:28], both[28:56])

    own = rows_of(fin)
    last.wait_recv()
    other = rows_of(fin_in)
    gk_out[...] = jnp.where(c == 0, own, other)
    gv_out[...] = jnp.where(c == 0, other, own)
    for run_ in runs + [run]:
        run_.finish()
    for copy in over + pairs + passed + [last] + [x for two in across for x in two]:
        copy.wait_send()


def reduce_call(own_code, sib_code, slots, ancx, wk, wv):
    hbm = pl.BlockSpec(memory_space=pl.ANY)
    smem = pl.BlockSpec(memory_space=pltpu.SMEM)
    vmem = pl.BlockSpec(memory_space=pltpu.VMEM)
    dma = pltpu.SemaphoreType.DMA
    sib = pltpu.VMEM((NA, BLK, HEAD), BF)
    xt = pltpu.VMEM((4, 2, OWN, HEAD), BF)
    return pl.pallas_call(
        reduce_kernel,
        out_shape=(
            jax.ShapeDtypeStruct((OWN, WIDTH), BF),
            jax.ShapeDtypeStruct((28, 512), F32),
            jax.ShapeDtypeStruct((28, 512), F32),
        ),
        in_specs=[smem, smem, vmem, vmem, hbm, hbm],
        out_specs=(vmem, vmem, vmem),
        scratch_shapes=[
            pltpu.VMEM((WIDTH, HEADS * HEAD), BF),
            pltpu.VMEM((WIDTH, HEADS * HEAD), BF),
            sib, sib, sib, sib,
            pltpu.VMEM((HEADS, 4, 4, 2, OWN, HEAD), BF),
            pltpu.VMEM((HEADS, 2, 2, 2, OWN, HEAD), BF),
            pltpu.VMEM((HEADS, 2, 4, 2, OWN, HEAD), BF),
            pltpu.VMEM((HEADS, 4, 2, OWN, HEAD), BF),
            pltpu.VMEM((HEADS, 2, OWN, HEAD), BF),
            pltpu.VMEM((HEADS, 2, 2, OWN, HEAD), BF),
            pltpu.VMEM((HEADS, 2, OWN, HEAD), BF),
            pltpu.VMEM((HEADS, OWN, HEAD), BF),
            xt, xt, xt, xt,
            pltpu.VMEM((16, 56, 512), F32),
            pltpu.VMEM((4, 4, 2, 64, 256), BF),
            pltpu.VMEM((2, 2, 2, 64, 256), BF),
            pltpu.VMEM((2, 4, 2, 64, 256), BF),
            pltpu.VMEM((4, 2, 64, 256), BF),
            pltpu.VMEM((2, 64, 256), BF),
            pltpu.VMEM((2, 2, 64, 256), BF),
            pltpu.VMEM((2, 64, 256), F32),
            pltpu.VMEM((2, 64, 256), F32),
            dma((2,)),
            dma((HEADS,)), dma((HEADS,)),
            dma((HEADS, 8)), dma((HEADS, 8)),
            dma((HEADS,)), dma((HEADS,)),
            dma((HEADS, 4)), dma((HEADS, 4)),
            dma((8,)), dma((8,)),
            dma((1,)), dma((1,)),
        ],
        compiler_params=pltpu.CompilerParams(
            collective_id=1, has_side_effects=True, vmem_limit_bytes=56 * MIB
        ),
        name="reduce_kv",
    )(own_code, sib_code, slots.reshape(HEADS, 2, NA, BLK, HEAD), ancx, wk, wv)


def on_device(q, bk, bv, out, grad, anc, wk, wv, blocks, count):
    slot = jnp.arange(NA, dtype=jnp.int32)
    leaves = jnp.arange(32, dtype=jnp.int32)
    code = jnp.where(
        (blocks[0][:, None] // 2 == leaves[None, :]) & (slot < count[0])[:, None],
        slot[:, None] * 4 + blocks[0][:, None] % 2 + 1,
        0,
    ).sum(axis=0, dtype=jnp.int32)
    sib_code = lax.ppermute(code, "leaf", [(i, i ^ 1) for i in range(32)])
    kvg, ancx = gather_call(anc, wk, wv)
    dq, slots, dbk, dbv = attend_call(blocks, count, kvg, q, out, grad, bk, bv)
    dstate, gk, gv = reduce_call(code, sib_code, slots, ancx, wk, wv)
    return dq, dbk, dbv, dstate, gk, gv


def solution(mesh):
    rows = P(("dp", "leaf"), None)
    return jax.shard_map(
        on_device,
        mesh=mesh,
        in_specs=(rows, rows, rows, rows, rows, rows, P(), P(), rows, P(("dp", "leaf"))),
        out_specs=(rows,) * 6,
        check_vma=False,
    )
```

time: 495 us -> 166 us (0.34); the launches traced: 486 us -> 166 us
  waiting for transfers between devices: 229 us -> 0.01 us
  Pallas kernels: 0 us -> 159 us
  matrix products: 114 us -> 0 us
  local copies, waits for them, and re-layouts: 99.7 us -> 4.01 us
  other arithmetic: 28.1 us -> 0.77 us
  between operations: 15.3 us -> 1.43 us
    pallas_call x0 -> x3, Pallas kernels: none -> 159 us  [the longest x1 64.4 us: reduce_call(): pl.pallas_call(reduce_kernel, out_shape=(jax.ShapeDtypeStruct((OWN, WIDTH...]
    unnamed x4 -> x0, waiting for transfers between devices: 134 us -> none
    dot_general x25 -> x0, matrix products: 114 us -> none  [the longest x9 41.2 us: contract_cols(): lax.dot_general(left, right, (((1,), (1,)), ((), ())), preferred_element_...]
    reduce_scatter x1 -> x0, waiting for transfers between devices: 94.4 us -> none  [on_device(): lax.psum_scatter(found.reshape(lax.axis_size('leaf') * (owned_blocks * BL...]
    slice x7 -> x0, local copies, waits for them, and re-layouts: 34.8 us -> none  [the longest x1 14.3 us: attend(): head_gradients[:, key_value_head]]
    convert_element_type x6 -> x0, local copies, waits for them, and re-layouts: 19.5 us -> none  [the longest x1 11.3 us: on_device(): found.reshape(lax.axis_size('leaf') * (owned_blocks * BLK), 2 * key_value...]
    reduce_sum x8 -> x1, other arithmetic: 18.9 us -> 0.09 us  [on_device(): code = jnp.where((blocks[0][:, None] // 2 == leaves[None, :]) & (slot < c...]
    reshape x8 -> x0, local copies, waits for them, and re-layouts: 18.2 us -> none  [the longest x4 7.27 us: attend(): grad_query.reshape(query_tokens, group_width * HEAD_SIZE)]
  transfers between devices with their start and end apart: 3 -> 1, of which waited for: 2 -> 0; matrix products, arithmetic and copies ran while one was open for 23% -> 0% of each run, Pallas kernels for 0% -> 57%
where the time goes in v1:
time: 166 us
  Pallas kernels  159 us (96%)
  local copies, waits for them, and re-layouts  4.01 us (2%)
    pallas_call x1, Pallas kernels, reduce_call(): pl.pallas_call(reduce_kernel, out_shape=(jax.ShapeDtypeStruct((OWN, WIDTH...  64.4 us
    pallas_call x1, Pallas kernels, attend_call(): pl.pallas_call(attend_kernel, grid=(HEADS,), out_shape=(jax.ShapeDtypeStr...  54.5 us
    pallas_call x1, Pallas kernels, gather_call(): pl.pallas_call(gather_kernel, out_shape=(jax.ShapeDtypeStruct((HEADS, 2,...  39.6 us
    unnamed x23, local copies, waits for them, and re-layouts  4.01 us
  transfers between devices with their start and end apart: 1, of which 0 were waited for; matrix products, arithmetic and copies ran while one was open for 0% of the time, Pallas kernels for 57%

profile of v1, /device:TPU:1, one launch (start us, length us, event | category | flops | bytes accessed | tf_op | source)
XLA Modules:
  0.0 166.2 jit_solution(13350892208594447682)
XLA Ops:
  1.3 0.7 and_select_fusion.1
  2.0 0.1 select_reduce_fusion.own_code
  2.0 0.0 copy-start.8
  2.1 0.0 copy-start
  2.1 0.0 copy-start.1
  2.1 0.0 copy-start.2
  2.1 0.0 copy-start.3
  2.1 0.0 copy-start.4
  2.1 0.0 copy-start.5
  2.1 1.5 collective-permute-start
  3.6 39.6 %gather_kv.1 = (bf16[4,2,4,4,2,128,128]{6,5,4,3,2,1,0:T(8,128)(2,1)}, bf16[4,2,128,896]{3,2,1,0:T(8,128)(2,1)}) custom-call(bf16[128,3584]{1,0:T(8,128)(2,1)} %anc_hbm.1, bf16[3584,512]{1,0:T(8,128)(2,1)} %wk_hbm.3, bf16[3584,512]{1,0:T(8,128)(2,1)} %wv_hbm.3), custom_call_target="tpu_custom_call" | custom-call | tf_op jit(solution)/shard_map/gather_kv/pallas_call | solution.py:198
  43.2 0.0 copy-done.8
  43.2 0.0 copy-done
  43.2 0.0 copy-done.1
  43.2 0.0 copy-done.2
  43.2 0.0 copy-done.3
  43.3 0.0 copy-done.4
  43.3 0.0 copy-done.5
  43.3 54.5 %attend.1 = (bf16[256,3584]{1,0:T(8,128)(2,1)}, bf16[4,2,1024,128]{3,2,1,0:T(8,128)(2,1)}, bf16[256,512]{1,0:T(8,128)(2,1)}, bf16[256,512]{1,0:T(8,128)(2,1)}) custom-call(s32[1,16]{1,0:T(1,128)S(1)} %copy-done.5, s32[1]{0:T(128)} %copy.19.count, bf16[4,2,64,64,128]{4,3,2,1,0:T(8,128)(2,1)} %bitcast.19, bf16[256,3584]{1,0:T(8,128)(2,1)S(1)} %copy-done, ...), custom_call_target="tpu_custom_call" | custom-call | tf_op jit(solution)/shard_map/attend/pallas_call | solution.py:304
  97.8 0.0 collective-permute-done.sib_code
  97.8 0.0 copy-start.9
  97.8 0.5 copy-done.9
  98.3 64.4 %reduce_kv.1 = (bf16[128,3584]{1,0:T(8,128)(2,1)}, f32[28,512]{1,0:T(8,128)}, f32[28,512]{1,0:T(8,128)}) custom-call(s32[32]{0:T(128)} %copy-done.8, s32[32]{0:T(128)} %copy-done.9, bf16[4,2,16,64,128]{4,3,2,1,0:T(8,128)(2,1)} %bitcast.20, bf16[4,2,128,896]{3,2,1,0:T(8,128)(2,1)} %get-tuple-element.20.ancx, bf16[3584,512]{1,0:T(8,128)(2,1)} %wk_hbm.3, ...), custom_call_target="tpu_custom_call" | custom-call | tf_op jit(solution)/shard_map/reduce_kv/pallas_call | solution.py:529
  162.7 0.0 copy-start.7
  162.7 0.0 copy-start.6
  162.8 2.2 %copy.20 = bf16[128,3584]{1,0:T(8,128)(2,1)} copy(bf16[128,3584]{1,0:T(8,128)(2,1)} %get-tuple-element.35) | data formatting | bytes 1835008
  165.0 0.0 copy-done.7
  165.0 0.6 copy.21
  165.6 0.0 copy-done.6
  165.6 0.6 copy.22
  (1 shorter events, 0.0 us)
Async XLA Ops:
  2.0 41.2 %copy-start.8 = (s32[32]{0:T(128)}, s32[32]{0:T(128)S(1)}, u32[]{:S(2)}) copy-start(s32[32]{0:T(128)S(1)} %select_reduce_fusion.own_code) | copy-start | bytes 388
  2.1 41.2 %copy-start = (bf16[256,3584]{1,0:T(8,128)(2,1)S(1)}, bf16[256,3584]{1,0:T(8,128)(2,1)}, u32[]{:S(2)}) copy-start(bf16[256,3584]{1,0:T(8,128)(2,1)} %q.1) | copy-start | bytes 5505028
  2.1 41.2 %copy-start.1 = (bf16[256,3584]{1,0:T(8,128)(2,1)S(1)}, bf16[256,3584]{1,0:T(8,128)(2,1)}, u32[]{:S(2)}) copy-start(bf16[256,3584]{1,0:T(8,128)(2,1)} %out.1) | copy-start | bytes 5505028
  2.1 41.2 %copy-start.2 = (bf16[256,3584]{1,0:T(8,128)(2,1)S(1)}, bf16[256,3584]{1,0:T(8,128)(2,1)}, u32[]{:S(2)}) copy-start(bf16[256,3584]{1,0:T(8,128)(2,1)} %grad.1) | copy-start | bytes 5505028
  2.1 41.2 %copy-start.3 = (bf16[256,512]{1,0:T(8,128)(2,1)S(1)}, bf16[256,512]{1,0:T(8,128)(2,1)}, u32[]{:S(2)}) copy-start(bf16[256,512]{1,0:T(8,128)(2,1)} %bk.1) | copy-start | bytes 786436
  2.1 41.2 %copy-start.4 = (bf16[256,512]{1,0:T(8,128)(2,1)S(1)}, bf16[256,512]{1,0:T(8,128)(2,1)}, u32[]{:S(2)}) copy-start(bf16[256,512]{1,0:T(8,128)(2,1)} %bv.1) | copy-start | bytes 786436
  2.1 41.2 %copy-start.5 = (s32[1,16]{1,0:T(1,128)S(1)}, s32[1,16]{1,0:T(1,128)}, u32[]{:S(2)}) copy-start(s32[1,16]{1,0:T(1,128)} %blocks.1) | copy-start | bytes 196
  2.1 95.7 %collective-permute-start = (s32[32]{0:T(128)S(1)}, s32[32]{0:T(128)S(1)}, u32[]{:S(2)}, u32[]{:S(2)}) collective-permute-start(s32[32]{0:T(128)S(1)} %select_reduce_fusion.own_code), channel_id=1, source_target_pairs={{0,1},{1,0},{2,3},{3,2},{4,5},{5,4},{6,7},{7,6},{8,9},{9,8},{10,11... | collective-permute-start | bytes 392 | tf_op jit(solution)/shard_map/ppermute | solution.py:583
  97.8 0.5 copy-start.9
  162.7 2.2 %copy-start.7 = (f32[28,512]{1,0:T(8,128)S(1)}, f32[28,512]{1,0:T(8,128)}, u32[]{:S(2)}) copy-start(f32[28,512]{1,0:T(8,128)} %get-tuple-element.36) | copy-start | bytes 172036
  162.7 2.8 %copy-start.6 = (f32[28,512]{1,0:T(8,128)S(1)}, f32[28,512]{1,0:T(8,128)}, u32[]{:S(2)}) copy-start(f32[28,512]{1,0:T(8,128)} %get-tuple-element.37) | copy-start | bytes 172036
